TPU v7x, 32 devices: a whole 2x2x4 slice. The times are simulated.
32 devices in a mesh: layer: 8 (over y, x, core), lat: 4 (over z).
Axes of the slice: x: 2, y: 2, z: 4, core: 2. Of those that a mesh axis runs over, the one named last changes fastest.
Arguments:
- saved_codes: bfloat16 [8, 512, 1024], P('layer', 'lat'), may hold values from 0.049804688 to 2
- relu_mask: int32 [8, 512, 1024], P('layer', 'lat'), may hold values 0 or 1
- errors: bfloat16 [8, 1024, 4096], P('layer'), may hold values from -0.29882812 to 0.29882812
- decoders: bfloat16 [8, 8, 512, 4096], P('layer', None, 'lat'), may hold values from -0.59765625 to 0.59765625
- inputs: bfloat16 [8, 1024, 4096], P('layer'), may hold values from -0.3984375 to 0.3984375
Outputs:
- decoder_grad: bfloat16 [8, 8, 512, 4096], P('layer', None, 'lat')
- code_grad: float32 [8, 512, 1024], P('layer', 'lat')
- encoder_grad: bfloat16 [8, 512, 4096], P('layer', 'lat')
All inputs are finite; a program needn't handle non-finite values. No bound on the sum of `relu_mask` on one device may be relied on, other than what follows from the above.
Results may differ from a plain program's by a relative error of at most 0.0049.
Values may be sent and summed in bfloat16 or wider, within the bound.
A program may use at most 128 MiB of HBM per device.

v0:
```python
import jax
import jax.numpy as jnp
from jax import lax
from jax.sharding import PartitionSpec as P


def body(saved_codes, relu_mask, errors, decoders, inputs):
    target = lax.axis_index("layer")
    target_error = errors[0]
    latents = saved_codes.shape[1]
    tokens = saved_codes.shape[2]
    model_width = target_error.shape[1]
    active = saved_codes * relu_mask.astype(jnp.bfloat16)
    gathered = lax.all_gather(active, "layer", axis=0, tiled=True)
    row_count = gathered.shape[0]
    allowed = (jnp.arange(row_count, dtype=jnp.int32) <= target)[:, None, None]

    def decoder_compute():
        products = jnp.dot(
            gathered.reshape(row_count * latents, tokens),
            target_error,
            preferred_element_type=jnp.float32,
        )
        products = products.reshape(row_count, latents, model_width)
        return jnp.where(allowed, products, 0.0).astype(jnp.bfloat16)

    def decoder_skipped():
        return jnp.zeros((row_count, latents, model_width), jnp.bfloat16)

    decoder_grad = lax.cond(jnp.int32(0) <= target, decoder_compute, decoder_skipped)
    code_row_count = 1 * lax.axis_size("layer")
    code_allowed = (jnp.arange(code_row_count, dtype=jnp.int32) <= target)[:, None, None]

    def code_compute():
        slab_rows = decoders[0]
        products = lax.dot_general(
            slab_rows.reshape(code_row_count * latents, model_width),
            target_error,
            (((1,), (1,)), ((), ())),
            preferred_element_type=jnp.float32,
        )
        products = products.reshape(code_row_count, latents, tokens)
        return jnp.where(code_allowed, products, 0.0)

    def code_skipped():
        return jnp.zeros((code_row_count, latents, tokens), jnp.float32)

    code_grad = lax.psum_scatter(
        lax.cond(jnp.int32(0) <= target, code_compute, code_skipped),
        "layer",
        scatter_dimension=0,
        tiled=True,
    )
    pre_grad = (code_grad[0] * relu_mask[0].astype(jnp.float32)).astype(jnp.bfloat16)
    encoder_grad = jnp.dot(pre_grad, inputs[0], preferred_element_type=jnp.float32).astype(
        jnp.bfloat16
    )
    return (decoder_grad[None], code_grad, encoder_grad[None])


def solution(mesh):
    return jax.shard_map(
        body,
        mesh=mesh,
        in_specs=(
            P("layer", "lat", None),
            P("layer", "lat", None),
            P("layer", None, None),
            P("layer", None, "lat", None),
            P("layer", None, None),
        ),
        out_specs=(P("layer", None, "lat", None), P("layer", "lat", None), P("layer", "lat", None)),
        check_vma=False,
    )
```

profile of v0, /device:TPU:13, one launch (start us, length us, event | category | flops | bytes accessed | tf_op | source)
XLA Modules:
  0.0 107.4 jit_solution(3927696207401091573)
XLA Ops:
  7.2 0.0 all-gather.2.cloned.1.call-start
  7.2 1.9 %convert_multiply_fusion = bf16[1,128,1024]{2,1,0:T(8,128)(2,1)} fusion(bf16[1,128,1024]{2,1,0:T(8,128)(2,1)} %param.9, s32[1,128,1024]{2,1,0:T(8,128)} %param.10), kind=kLoop, calls=%fused_computation.14 | loop fusion | flops 262144 | bytes 1048576 | tf_op jit(solution)/shard_map/mul | solution.py:13
  9.1 0.0 all-gather.2.cloned.1.call-update
  9.1 0.0 reduce-scatter.2.cloned.1.call-start
  9.2 15.1 %conditional.3 = (f32[8,128,1024]{2,1,0:T(8,128)}) conditional(s32[]{:T(128)} %convert_element_type.23, () %tuple.24, (pred[8,1,1]{0,2,1:T(4,128)(4,1)S(1)}, bf16[1,8,128,4096]{3,2,1,0:T(8,128)(2,1)}, bf16[1024,4096]{1,0:T(8,128)(2,1)}) %tuple.35), branch_computations={%region_2.3_spmd, %region_3.4_spmd} | conditional | flops 8590983168 | bytes 20971536 | solution.py:49
  9.2 15.1 %fusion.8 = f32[8,128,1024]{2,1,0:T(8,128)} fusion(bf16[1024,4096]{1,0:T(8,128)(2,1)} %get-tuple-element.24, bf16[1,8,128,4096]{3,2,1,0:T(8,128)(2,1)} %get-tuple-element.29, pred[8]{0:T(512)(128)(4,1)S(1)} %bitcast.35), kind=kOutput, calls=%fused_computation.7 | convolution fusion | flops 8590983168 | bytes 20971528 | tf_op jit(solution)/shard_map/cond/branch_1_fun/dot_general | solution.py:36
  24.3 0.0 reduce-scatter.2.cloned.1.call-update
  24.3 15.6 %all-gather.2.cloned.1.call-done = bf16[8,128,1024]{2,1,0:T(8,128)(2,1)} async-done(((bf16[1,128,1024]{2,1,0:T(8,128)(2,1)}), bf16[8,128,1024]{2,1,0:T(8,128)(2,1)}) %all-gather.2.cloned.1.call-update) | async-done | bytes 2097168 | tf_op jit(solution)/shard_map/all_gather | solution.py:14
  39.8 0.0 copy-start
  39.8 14.8 %conditional.2 = (bf16[1,8,128,4096]{3,2,1,0:T(8,128)(2,1)}) conditional(s32[]{:T(128)} %convert_element_type.23, () %tuple.22, (pred[8,1,1]{0,2,1:T(4,128)(4,1)S(1)}, bf16[8,128,1024]{2,1,0:T(8,128)(2,1)}, bf16[1024,4096]{1,0:T(8,128)(2,1)}) %tuple.36), branch_computations={%region_0.0_spmd, %region_1.2_spmd} | conditional | flops 8598323200 | bytes 18874384 | solution.py:30
  39.8 14.8 %fusion = bf16[1,8,128,4096]{3,2,1,0:T(8,128)(2,1)} fusion(pred[8]{0:T(512)(128)(4,1)S(1)} %bitcast.36, bf16[8,128,1024]{2,1,0:T(8,128)(2,1)} %get-tuple-element.20, bf16[1024,4096]{1,0:T(8,128)(2,1)} %get-tuple-element.21), kind=kOutput, calls=%fused_computation.1 | convolution fusion | flops 8598323200 | bytes 18874376 | tf_op jit(solution)/shard_map/cond/branch_1_fun/dot_general | solution.py:19
  54.6 40.1 %reduce-scatter.2.cloned.1.call-done = f32[1,128,1024]{2,1,0:T(8,128)} async-done(((f32[8,128,1024]{2,1,0:T(8,128)}), f32[1,128,1024]{2,1,0:T(8,128)}) %reduce-scatter.2.cloned.1.call-update) | async-done | bytes 524304 | tf_op jit(solution)/shard_map/reduce_scatter | solution.py:48
  94.8 0.0 copy-done
  94.8 5.8 %fusion.18 = bf16[1,128,4096]{2,1,0:T(8,128)(2,1)} fusion(bf16[1,1024,4096]{2,1,0:T(8,128)(2,1)} %param.13, f32[1,128,1024]{2,1,0:T(8,128)} %reduce-scatter.2.cloned.1.call-done, s32[1,128,1024]{2,1,0:T(8,128)S(1)} %copy-done), kind=kOutput, calls=%fused_computation.11 | convolution fusion | flops 1074659328 | bytes 10485760 | tf_op jit(solution)/shard_map/dot_general | solution.py:55
  (1 shorter events, 0.0 us)
Async XLA Ops:
  7.2 32.7 %all-gather.2.cloned.1.call-start = ((), (), s32[]{:S(2)}) async-start(), calls=%async_computation.1 | async-start | bytes 2359296 | tf_op jit(solution)/shard_map/all_gather | solution.py:14
  9.1 85.7 %reduce-scatter.2.cloned.1.call-start = ((), (), s32[]{:S(2)}) async-start(), calls=%async_computation.2 | async-start | bytes 4718592 | tf_op jit(solution)/shard_map/reduce_scatter | solution.py:48
  39.8 54.9 %copy-start = (s32[1,128,1024]{2,1,0:T(8,128)S(1)}, s32[1,128,1024]{2,1,0:T(8,128)}, u32[]{:S(2)}) copy-start(s32[1,128,1024]{2,1,0:T(8,128)} %param.10) | copy-start | bytes 1572868
Sparse Core Ops, SparseCore 0:
  10.5 29.3 all-gather.1
  43.8 50.9 reduce-scatter.1
where the time goes:
time: 109 us; the launch traced here: 107 us
  waiting for transfers between devices  55.7 us (51%)
  matrix products  35.7 us (33%)
  between operations  14 us (13%)
  other arithmetic  1.87 us (2%)
    reduce_scatter x1, waiting for transfers between devices, body(): lax.psum_scatter(lax.cond(jnp.int32(0) <= target, code_compute, code_skip...  40.1 us
    all_gather x1, waiting for transfers between devices, body(): gathered = lax.all_gather(active, 'layer', axis=0, tiled=True)  15.6 us
    dot_general x1, matrix products, code_compute(): lax.dot_general(slab_rows.reshape(code_row_count * latents, model_width),...  15.1 us
    dot_general x1, matrix products, decoder_compute(): jnp.dot(gathered.reshape(row_count * latents, tokens), target_error, pref...  14.8 us
    dot_general x1, matrix products, body(): jnp.dot(pre_grad, inputs[0], preferred_element_type=jnp.float32)  5.8 us
  transfers between devices with their start and end apart: 2, of which 2 were waited for; matrix products, arithmetic and copies ran while one was open for 28% of the time, Pallas kernels for 0%

commit v1 on v0

v1 whole, which is shorter than its diff:
```python
import functools

import jax
import jax.numpy as jnp
from jax import lax
from jax.experimental import pallas as pl
from jax.experimental.pallas import tpu as pltpu
from jax.sharding import PartitionSpec as P

MESH = pl.DeviceIdType.MESH
CHUNKS = 4
DEPTHS = 4
MIB = 1 << 20


def exchange_kernel(
    n, codes_hbm, mask_hbm, errors_hbm, decoders_hbm, gathered, code_grad,
    codes, mask, active, errors, decoders, terms, twin_terms, outgoing, incoming,
    load_sem, decoder_sem, error_sem, own_sem,
    gather_send, gather_recv, relay_send, relay_recv,
    twin_send, twin_recv, term_send, term_recv,
):
    me = lax.axis_index("layer")
    core = lax.rem(me, 2)
    chip = me // 2
    twin = me + 1 - 2 * core
    chips = n // 2
    latents, tokens = active.shape
    width = errors.shape[1]
    token_chunk = tokens // CHUNKS
    depth = width // DEPTHS

    load_codes = pltpu.make_async_copy(codes_hbm, codes, load_sem.at[0])
    load_mask = pltpu.make_async_copy(mask_hbm, mask, load_sem.at[1])

    def load_errors(j):
        rows = pl.ds(pl.multiple_of(j * token_chunk, token_chunk), token_chunk)
        return pltpu.make_async_copy(errors_hbm.at[rows], errors.at[rows], error_sem.at[j])

    def load_decoders(k):
        columns = pl.ds(k * depth, depth)
        return pltpu.make_async_copy(decoders_hbm.at[:, columns], decoders.at[:, columns], decoder_sem.at[k])

    load_codes.start()
    load_mask.start()
    load_errors(0).start()
    for k in range(DEPTHS):
        load_decoders(k).start()
    for j in range(1, CHUNKS):
        load_errors(j).start()

    barrier = pltpu.get_barrier_semaphore()
    pl.semaphore_signal(barrier, inc=1, device_id={"layer": twin}, device_id_type=MESH)
    for other in range(chips):
        @pl.when(other != chip)
        def _():
            pl.semaphore_signal(barrier, inc=1, device_id={"layer": 2 * other + core}, device_id_type=MESH)

    load_codes.wait()
    load_mask.wait()
    active[...] = codes[...] * mask[...].astype(jnp.bfloat16)
    keep = pltpu.make_async_copy(active, gathered.at[me], own_sem)
    keep.start()
    pl.semaphore_wait(barrier, chips)

    def send_active(other):
        return pltpu.make_async_remote_copy(
            src_ref=active, dst_ref=gathered.at[me],
            send_sem=gather_send.at[other], recv_sem=gather_recv.at[chip],
            device_id={"layer": 2 * other + core}, device_id_type=MESH,
        )

    def take_active(source):
        return pltpu.make_async_remote_copy(
            src_ref=active, dst_ref=gathered.at[2 * source + core],
            send_sem=gather_send.at[source], recv_sem=gather_recv.at[source],
            device_id={"layer": 2 * source + core}, device_id_type=MESH,
        )

    def relay(source):
        place = gathered.at[2 * source + core]
        return pltpu.make_async_remote_copy(
            src_ref=place, dst_ref=place,
            send_sem=relay_send.at[source], recv_sem=relay_recv.at[source],
            device_id={"layer": twin}, device_id_type=MESH,
        )

    def take_relay(source):
        place = gathered.at[2 * source + 1 - core]
        return pltpu.make_async_remote_copy(
            src_ref=place, dst_ref=place,
            send_sem=relay_send.at[source], recv_sem=relay_recv.at[source],
            device_id={"layer": twin}, device_id_type=MESH,
        )

    own_to_twin = pltpu.make_async_remote_copy(
        src_ref=active, dst_ref=gathered.at[me],
        send_sem=relay_send.at[chip], recv_sem=relay_recv.at[chip],
        device_id={"layer": twin}, device_id_type=MESH,
    )
    for other in reversed(range(chips)):
        @pl.when(other > chip)
        def _():
            send_active(other).start()

    own_to_twin.start()

    def send_twin(j):
        return pltpu.make_async_remote_copy(
            src_ref=terms.at[j, 1 - core], dst_ref=twin_terms.at[j],
            send_sem=twin_send.at[j], recv_sem=twin_recv.at[j],
            device_id={"layer": twin}, device_id_type=MESH,
        )

    def send_term(j, other):
        return pltpu.make_async_remote_copy(
            src_ref=outgoing.at[j, other], dst_ref=incoming.at[j, chip],
            send_sem=term_send.at[j, other], recv_sem=term_recv.at[j, chip],
            device_id={"layer": 2 * other + core}, device_id_type=MESH,
        )

    def take_term(j, source):
        return pltpu.make_async_remote_copy(
            src_ref=outgoing.at[j, source], dst_ref=incoming.at[j, source],
            send_sem=term_send.at[j, source], recv_sem=term_recv.at[j, source],
            device_id={"layer": 2 * source + core}, device_id_type=MESH,
        )

    def pair_sum(j):
        send_twin(j).wait_recv()
        for other in range(chips):
            @pl.when(other < chip)
            def _():
                total = terms[j, core, other] + twin_terms[j, other]
                outgoing[j, other] = total.astype(jnp.bfloat16)
                send_term(j, other).start()

    @pl.loop(0, CHUNKS)
    def _(j):
        load_errors(j).wait()
        rows = pl.ds(pl.multiple_of(j * token_chunk, token_chunk), token_chunk)
        for k in range(DEPTHS):
            @pl.when(j == 0)
            def _():
                load_decoders(k).wait()
            columns = pl.ds(k * depth, depth)
            product = lax.dot_general(
                decoders[:, columns], errors[rows, columns],
                (((1,), (1,)), ((), ())),
                preferred_element_type=jnp.float32,
            ).reshape(chips, 2, latents, token_chunk)
            for parity in range(2):
                if k == 0:
                    terms[j, parity] = product[:, parity]
                else:
                    terms[j, parity] += product[:, parity]
        send_twin(j).start()

        @pl.when(j >= 1)
        def _():
            pair_sum(j - 1)

        @pl.when(j == CHUNKS - 2)
        def _():
            for source in range(chips):
                @pl.when(source == chip - 1)
                def _():
                    take_active(source).wait_recv()
                    relay(source).start()

    for source in range(chips):
        @pl.when(source < chip - 1)
        def _():
            take_active(source).wait_recv()
            relay(source).start()

    pair_sum(CHUNKS - 1)

    for j in range(CHUNKS):
        columns = pl.ds(j * token_chunk, token_chunk)
        own = terms[j, core, chip]
        code_grad[:, columns] = jnp.where(core == 0, own + twin_terms[j, chip], own)
        for source in range(chips):
            @pl.when(source > chip)
            def _():
                take_term(j, source).wait_recv()
                code_grad[:, columns] += incoming[j, source].astype(jnp.float32)

    keep.wait()
    own_to_twin.wait_send()
    take_relay(chip).wait_recv()
    for other in range(chips):
        @pl.when(other < chip)
        def _():
            relay(other).wait_send()
            take_relay(other).wait_recv()
            for j in range(CHUNKS):
                send_term(j, other).wait_send()

        @pl.when(other > chip)
        def _():
            send_active(other).wait_send()

    for j in range(CHUNKS):
        send_twin(j).wait_send()


def exchange(n, codes, mask, errors, decoders):
    latents, tokens = codes.shape
    width = errors.shape[1]
    chips = n // 2
    token_chunk = tokens // CHUNKS
    any_space = pl.BlockSpec(memory_space=pl.ANY)
    dma = pltpu.SemaphoreType.DMA
    return pl.pallas_call(
        functools.partial(exchange_kernel, n),
        out_shape=(
            jax.ShapeDtypeStruct((n, latents, tokens), jnp.bfloat16),
            jax.ShapeDtypeStruct((latents, tokens), jnp.float32),
        ),
        in_specs=[any_space] * 4,
        out_specs=(any_space, pl.BlockSpec(memory_space=pltpu.VMEM)),
        scratch_shapes=[
            pltpu.VMEM((latents, tokens), jnp.bfloat16),
            pltpu.VMEM((latents, tokens), jnp.int32),
            pltpu.VMEM((latents, tokens), jnp.bfloat16),
            pltpu.VMEM((tokens, width), jnp.bfloat16),
            pltpu.VMEM((n * latents, width), jnp.bfloat16),
            pltpu.VMEM((CHUNKS, 2, chips, latents, token_chunk), jnp.float32),
            pltpu.VMEM((CHUNKS, chips, latents, token_chunk), jnp.float32),
            pltpu.VMEM((CHUNKS, chips, latents, token_chunk), jnp.bfloat16),
            pltpu.VMEM((CHUNKS, chips, latents, token_chunk), jnp.bfloat16),
            dma((2,)), dma((DEPTHS,)), dma((CHUNKS,)), dma,
            dma((chips,)), dma((chips,)), dma((chips,)), dma((chips,)),
            dma((CHUNKS,)), dma((CHUNKS,)), dma((CHUNKS, chips)), dma((CHUNKS, chips)),
        ],
        compiler_params=pltpu.CompilerParams(
            collective_id=0, has_side_effects=True, vmem_limit_bytes=48 * MIB
        ),
        cost_estimate=pl.CostEstimate(
            flops=2 * n * latents * tokens * width,
            bytes_accessed=2 * (n * latents + tokens) * width,
            transcendentals=0,
        ),
        name="exchange",
    )(codes, mask, errors, decoders)


def gradients_kernel(n, gathered, code, mask, errors, inputs, decoder_grad, code_grad, encoder_grad, pre):
    me = lax.axis_index("layer")
    latents = code.shape[0]
    columns = errors.shape[1]
    half = n // 2

    @pl.when(pl.program_id(0) == 0)
    def _():
        code_grad[...] = code[...]
        pre[...] = (code[...] * mask[...].astype(jnp.float32)).astype(jnp.bfloat16)

    def rows(first):
        products = jnp.dot(
            gathered[pl.ds(first * latents, half * latents)], errors[...],
            preferred_element_type=jnp.float32,
        ).reshape(half, latents, columns)
        for s in range(half):
            allowed = first + s <= me
            decoder_grad[first + s] = jnp.where(allowed, products[s], 0.0).astype(jnp.bfloat16)

    rows(0)

    @pl.when(me >= half)
    def _():
        rows(half)

    @pl.when(me < half)
    def _():
        decoder_grad[half:] = jnp.zeros((n - half, latents, columns), jnp.bfloat16)

    encoder_grad[...] = jnp.dot(
        pre[...], inputs[...], preferred_element_type=jnp.float32
    ).astype(jnp.bfloat16)


def gradients(n, gathered, code, mask, errors, inputs):
    latents, tokens = code.shape
    width = errors.shape[1]
    columns = min(512, width)
    whole = lambda *shape: pl.BlockSpec(shape, lambda i: (0,) * len(shape))
    return pl.pallas_call(
        functools.partial(gradients_kernel, n),
        grid=(width // columns,),
        out_shape=(
            jax.ShapeDtypeStruct((n, latents, width), jnp.bfloat16),
            jax.ShapeDtypeStruct((latents, tokens), jnp.float32),
            jax.ShapeDtypeStruct((latents, width), jnp.bfloat16),
        ),
        in_specs=[
            whole(n * latents, tokens),
            whole(latents, tokens),
            whole(latents, tokens),
            pl.BlockSpec((tokens, columns), lambda i: (0, i)),
            pl.BlockSpec((tokens, columns), lambda i: (0, i)),
        ],
        out_specs=(
            pl.BlockSpec((n, latents, columns), lambda i: (0, 0, i)),
            whole(latents, tokens),
            pl.BlockSpec((latents, columns), lambda i: (0, i)),
        ),
        scratch_shapes=[pltpu.VMEM((latents, tokens), jnp.bfloat16)],
        compiler_params=pltpu.CompilerParams(vmem_limit_bytes=40 * MIB),
        cost_estimate=pl.CostEstimate(
            flops=2 * (n + 1) * latents * tokens * width,
            bytes_accessed=2 * (n * latents + 2 * tokens) * width,
            transcendentals=0,
        ),
        name="gradients",
    )(gathered, code, mask, errors, inputs)


def body(saved_codes, relu_mask, errors, decoders, inputs, n):
    latents = saved_codes.shape[1]
    tokens = saved_codes.shape[2]
    width = errors.shape[2]
    gathered, code = exchange(
        n, saved_codes[0], relu_mask[0], errors[0], decoders.reshape(n * latents, width)
    )
    decoder_grad, code_grad, encoder_grad = gradients(
        n, gathered.reshape(n * latents, tokens), code, relu_mask[0], errors[0], inputs[0]
    )
    return decoder_grad[None], code_grad[None], encoder_grad[None]


def solution(mesh):
    return jax.shard_map(
        functools.partial(body, n=mesh.shape["layer"]),
        mesh=mesh,
        in_specs=(
            P("layer", "lat", None),
            P("layer", "lat", None),
            P("layer", None, None),
            P("layer", None, "lat", None),
            P("layer", None, None),
        ),
        out_specs=(P("layer", None, "lat", None), P("layer", "lat", None), P("layer", "lat", None)),
        check_vma=False,
    )
```

time: 109 us -> 50.4 us (0.46)
  the two profiles are of different devices: /device:TPU:13 before, /device:TPU:20 now
where the time goes in v1:
time: 50.4 us; the launch traced here: 50 us
  Pallas kernels  47.3 us (94%)
  local copies, waits for them, and re-layouts  1.99 us (4%)
  between operations  0.67 us (1%)
    pallas_call x1, Pallas kernels, exchange(): pl.pallas_call(functools.partial(exchange_kernel, n), out_shape=(jax.Shap...  30.4 us
    pallas_call x1, Pallas kernels, gradients(): pl.pallas_call(functools.partial(gradients_kernel, n), grid=(width // col...  16.9 us
    unnamed x8, local copies, waits for them, and re-layouts  1.99 us

profile of v1, /device:TPU:20, one launch (start us, length us, event | category | flops | bytes accessed | tf_op | source)
XLA Modules:
  0.0 50.0 jit_solution(12045122690723449543)
XLA Ops:
  0.6 0.0 copy-start.1
  0.6 1.0 %copy-done.1 = s32[1,128,1024]{2,1,0:T(8,128)S(1)} copy-done((s32[1,128,1024]{2,1,0:T(8,128)S(1)}, s32[1,128,1024]{2,1,0:T(8,128)}, u32[]{:S(2)}) %copy-start.1) | copy-done | bytes 524312
  1.7 0.0 copy-start.3
  1.7 0.9 %copy-done.3 = bf16[1,128,1024]{2,1,0:T(8,128)(2,1)S(1)} copy-done((bf16[1,128,1024]{2,1,0:T(8,128)(2,1)S(1)}, bf16[1,128,1024]{2,1,0:T(8,128)(2,1)}, u32[]{:S(2)}) %copy-start.3) | copy-done | bytes 262168
  2.6 0.0 copy-start
  2.6 0.0 copy-start.2
  2.6 30.4 %exchange.1 = (bf16[8,128,1024]{2,1,0:T(8,128)(2,1)S(1)}, f32[128,1024]{1,0:T(8,128)S(1)}) custom-call(bf16[128,1024]{1,0:T(8,128)(2,1)S(1)} %bitcast.13, s32[128,1024]{1,0:T(8,128)S(1)} %bitcast.11, bf16[1024,4096]{1,0:T(8,128)(2,1)} %bitcast.9, bf16[1024,4096]{1,0:T(8,128)(2,1)} %bitcast.15), custom_call_target="tpu_custom_call" | custom-call | flops 8589934592 | bytes 16777216 | tf_op jit(solution)/shard_map/exchange/pallas_call | solution.py:215
  33.1 0.0 copy-done
  33.1 0.0 copy-done.2
  33.1 16.9 %gradients.1 = (bf16[8,128,4096]{2,1,0:T(8,128)(2,1)}, f32[128,1024]{1,0:T(8,128)}, bf16[128,4096]{1,0:T(8,128)(2,1)}) custom-call(bf16[1024,1024]{1,0:T(8,128)(2,1)S(1)} %bitcast.14, f32[128,1024]{1,0:T(8,128)S(1)} %get-tuple-element.9.code, s32[128,1024]{1,0:T(8,128)S(1)} %bitcast.12, bf16[1024,4096]{1,0:T(8,128)(2,1)S(1)} %bitcast.10, ...), custom_call_target="tpu_custom_call" | custom-call | flops 9663676416 | bytes 25165824 | tf_op jit(solution)/shard_map/gradients/pallas_call | solution.py:289
Async XLA Ops:
  0.6 1.0 %copy-start.1 = (s32[1,128,1024]{2,1,0:T(8,128)S(1)}, s32[1,128,1024]{2,1,0:T(8,128)}, u32[]{:S(2)}) copy-start(s32[1,128,1024]{2,1,0:T(8,128)} %param.6) | copy-start | bytes 1572868
  1.7 0.9 %copy-start.3 = (bf16[1,128,1024]{2,1,0:T(8,128)(2,1)S(1)}, bf16[1,128,1024]{2,1,0:T(8,128)(2,1)}, u32[]{:S(2)}) copy-start(bf16[1,128,1024]{2,1,0:T(8,128)(2,1)} %param.5) | copy-start | bytes 786436
  2.6 30.4 %copy-start = (bf16[1,1024,4096]{2,1,0:T(8,128)(2,1)S(1)}, bf16[1,1024,4096]{2,1,0:T(8,128)(2,1)}, u32[]{:S(2)}) copy-start(bf16[1,1024,4096]{2,1,0:T(8,128)(2,1)} %param.7) | copy-start | bytes 25165828
  2.6 30.4 %copy-start.2 = (s32[1,128,1024]{2,1,0:T(8,128)S(1)}, s32[1,128,1024]{2,1,0:T(8,128)}, u32[]{:S(2)}) copy-start(s32[1,128,1024]{2,1,0:T(8,128)} %param.6) | copy-start | bytes 1572868

commit v2 on v1

v2 whole, which is shorter than its diff:
```python
import functools

import jax
import jax.numpy as jnp
from jax import lax
from jax.experimental import pallas as pl
from jax.experimental.pallas import tpu as pltpu
from jax.sharding import PartitionSpec as P

MESH = pl.DeviceIdType.MESH
DEPTHS = 4
COLUMNS = 512
MIB = 1 << 20


def exchange_kernel(
    n, codes_hbm, mask_hbm, errors_hbm, decoders_hbm, decoder_grad, code_grad,
    codes, mask, gathered, errors, decoders, terms, twin_terms, outgoing, incoming, stage,
    load_sem, decoder_sem, error_sem, stage_sem,
    gather_send, gather_recv, relay_send, relay_recv,
    twin_send, twin_recv, term_send, term_recv,
):
    me = lax.axis_index("layer")
    core = lax.rem(me, 2)
    chip = me // 2
    twin = me + 1 - 2 * core
    chips = n // 2
    group = chips // 2
    late = chip >= group
    _, latents, tokens = gathered.shape
    width = errors.shape[1]
    half_rows = 2 * group * latents
    half_tokens = tokens // 2
    depth = width // DEPTHS

    load_codes = pltpu.make_async_copy(codes_hbm, codes, load_sem.at[0])
    load_mask = pltpu.make_async_copy(mask_hbm, mask, load_sem.at[1])

    def load_errors(k):
        part = (pl.ds(half_tokens, half_tokens), slice(None))
        if k < DEPTHS:
            part = (pl.ds(0, half_tokens), pl.ds(k * depth, depth))
        return pltpu.make_async_copy(errors_hbm.at[part], errors.at[part], error_sem.at[k])

    def load_decoders(k):
        part = (pl.ds(half_rows, half_rows), slice(None))
        if k < DEPTHS:
            part = (pl.ds(0, half_rows), pl.ds(k * depth, depth))
        return pltpu.make_async_copy(decoders_hbm.at[part], decoders.at[part], decoder_sem.at[k])

    load_codes.start()
    load_mask.start()
    for k in range(DEPTHS):
        load_errors(k).start()
        load_decoders(k).start()
    load_errors(DEPTHS).start()

    @pl.when(late)
    def _():
        load_decoders(DEPTHS).start()

    barrier = pltpu.get_barrier_semaphore()
    pl.semaphore_signal(barrier, inc=1, device_id={"layer": twin}, device_id_type=MESH)
    for other in range(chips):
        @pl.when(other != chip)
        def _():
            pl.semaphore_signal(barrier, inc=1, device_id={"layer": 2 * other + core}, device_id_type=MESH)

    load_codes.wait()
    load_mask.wait()
    gathered[me] = codes[...] * mask[...].astype(jnp.bfloat16)
    pl.semaphore_wait(barrier, chips)

    def send_active(other):
        return pltpu.make_async_remote_copy(
            src_ref=gathered.at[me], dst_ref=gathered.at[me],
            send_sem=gather_send.at[other], recv_sem=gather_recv.at[chip],
            device_id={"layer": 2 * other + core}, device_id_type=MESH,
        )

    def take_active(source):
        place = gathered.at[2 * source + core]
        return pltpu.make_async_remote_copy(
            src_ref=place, dst_ref=place,
            send_sem=gather_send.at[source], recv_sem=gather_recv.at[source],
            device_id={"layer": 2 * source + core}, device_id_type=MESH,
        )

    def relay(source):
        place = gathered.at[2 * source + core]
        return pltpu.make_async_remote_copy(
            src_ref=place, dst_ref=place,
            send_sem=relay_send.at[source], recv_sem=relay_recv.at[source],
            device_id={"layer": twin}, device_id_type=MESH,
        )

    def take_relay(source):
        place = gathered.at[2 * source + 1 - core]
        return pltpu.make_async_remote_copy(
            src_ref=place, dst_ref=place,
            send_sem=relay_send.at[source], recv_sem=relay_recv.at[source],
            device_id={"layer": twin}, device_id_type=MESH,
        )

    for other in reversed(range(chips)):
        @pl.when(other > chip)
        def _():
            send_active(other).start()

    relay(chip).start()

    def send_twin(m):
        return pltpu.make_async_remote_copy(
            src_ref=terms.at[m, 1 - core], dst_ref=twin_terms.at[m],
            send_sem=twin_send.at[m], recv_sem=twin_recv.at[m],
            device_id={"layer": twin}, device_id_type=MESH,
        )

    def send_term(m, place):
        target = (m // 2) * group + place
        return pltpu.make_async_remote_copy(
            src_ref=outgoing.at[m, place], dst_ref=incoming.at[lax.rem(m, 2), chip],
            send_sem=term_send.at[m, place], recv_sem=term_recv.at[lax.rem(m, 2), chip],
            device_id={"layer": 2 * target + core}, device_id_type=MESH,
        )

    def take_term(q, source):
        return pltpu.make_async_remote_copy(
            src_ref=incoming.at[q, source], dst_ref=incoming.at[q, source],
            send_sem=term_send.at[0, 0], recv_sem=term_recv.at[q, source],
            device_id={"layer": 2 * source + core}, device_id_type=MESH,
        )

    def pair_sum(m):
        send_twin(m).wait_recv()
        for place in range(group):
            @pl.when((m // 2) * group + place < chip)
            def _():
                total = terms[m, core, place] + twin_terms[m, place]
                outgoing[m, place] = total.astype(jnp.bfloat16)
                send_term(m, place).start()

    steps = jnp.where(late, 4, 2)

    @pl.loop(0, steps)
    def _(m):
        @pl.when(m == 1)
        def _():
            load_errors(DEPTHS).wait()

        @pl.when(m == 2)
        def _():
            load_decoders(DEPTHS).wait()

        rows = pl.ds(pl.multiple_of((m // 2) * half_rows, half_rows), half_rows)
        part = pl.ds(pl.multiple_of(lax.rem(m, 2) * half_tokens, half_tokens), half_tokens)
        for k in range(DEPTHS):
            @pl.when(m == 0)
            def _():
                load_errors(k).wait()
                load_decoders(k).wait()

            columns = pl.ds(k * depth, depth)
            product = lax.dot_general(
                decoders[rows, columns], errors[part, columns],
                (((1,), (1,)), ((), ())),
                preferred_element_type=jnp.float32,
            ).reshape(group, 2, latents, half_tokens)
            for parity in range(2):
                if k == 0:
                    terms[m, parity] = product[:, parity]
                else:
                    terms[m, parity] += product[:, parity]
        send_twin(m).start()

        @pl.when(m >= 1)
        def _():
            pair_sum(m - 1)

        @pl.when(m == 1)
        def _():
            for source in range(chips):
                @pl.when(source == chip - 1)
                def _():
                    take_active(source).wait_recv()
                    relay(source).start()

    blocks = width // COLUMNS

    def put(first, i, slot):
        columns = pl.ds(pl.multiple_of(i * COLUMNS, COLUMNS), COLUMNS)
        return pltpu.make_async_copy(
            stage.at[slot], decoder_grad.at[pl.ds(first, 2 * group), :, columns], stage_sem.at[slot]
        )

    def decoder_rows(first, late_sum):
        @pl.loop(0, blocks)
        def _(i):
            slot = lax.rem(i, 2)

            @pl.when(i >= 2)
            def _():
                put(first, i - 2, slot).wait()

            columns = pl.ds(pl.multiple_of(i * COLUMNS, COLUMNS), COLUMNS)
            products = jnp.dot(
                gathered[first:first + 2 * group].reshape(half_rows, tokens), errors[:, columns],
                preferred_element_type=jnp.float32,
            ).reshape(2 * group, latents, COLUMNS)
            for s in range(2 * group):
                stage[slot, s] = jnp.where(first + s <= me, products[s], 0.0).astype(jnp.bfloat16)
            put(first, i, slot).start()
            if late_sum:
                @pl.when(i == 0)
                def _():
                    pair_sum(3)

        put(first, blocks - 2, (blocks - 2) % 2).wait()
        put(first, blocks - 1, (blocks - 1) % 2).wait()

    @pl.when(jnp.logical_not(late))
    def _():
        pair_sum(1)
        stage[0] = jnp.zeros(stage.shape[1:], stage.dtype)
        for i in range(blocks):
            put(2 * group, i, 0).start()

    for source in range(chips):
        @pl.when(source < chip - 1)
        def _():
            take_active(source).wait_recv()
            relay(source).start()

    take_relay(chip).wait_recv()

    @pl.when(late)
    def _():
        for source in range(group, chips):
            @pl.when(source < chip)
            def _():
                take_relay(source).wait_recv()
        decoder_rows(2 * group, True)

    @pl.when(jnp.logical_not(late))
    def _():
        for i in range(blocks):
            put(2 * group, i, 0).wait()

    for source in range(group):
        @pl.when(source < chip)
        def _():
            take_relay(source).wait_recv()
    decoder_rows(0, False)

    half = chip // group
    place = lax.rem(chip, group)
    for q in range(2):
        columns = pl.ds(q * half_tokens, half_tokens)
        own = terms[2 * half + q, core, place]
        code_grad[:, columns] = jnp.where(core == 0, own + twin_terms[2 * half + q, place], own)
        for source in range(chips):
            @pl.when(source > chip)
            def _():
                take_term(q, source).wait_recv()
                code_grad[:, columns] += incoming[q, source].astype(jnp.float32)

    relay(chip).wait_send()
    for other in range(chips):
        @pl.when(other < chip)
        def _():
            relay(other).wait_send()
            for q in range(2):
                send_term(2 * (other // group) + q, other % group).wait_send()

        @pl.when(other > chip)
        def _():
            send_active(other).wait_send()

    for m in range(2):
        send_twin(m).wait_send()

    @pl.when(late)
    def _():
        for m in range(2, 4):
            send_twin(m).wait_send()


def exchange(n, codes, mask, errors, decoders):
    latents, tokens = codes.shape
    width = errors.shape[1]
    chips = n // 2
    group = chips // 2
    half_tokens = tokens // 2
    any_space = pl.BlockSpec(memory_space=pl.ANY)
    dma = pltpu.SemaphoreType.DMA
    return pl.pallas_call(
        functools.partial(exchange_kernel, n),
        out_shape=(
            jax.ShapeDtypeStruct((n, latents, width), jnp.bfloat16),
            jax.ShapeDtypeStruct((latents, tokens), jnp.float32),
        ),
        in_specs=[any_space] * 4,
        out_specs=(any_space, pl.BlockSpec(memory_space=pltpu.VMEM)),
        scratch_shapes=[
            pltpu.VMEM((latents, tokens), jnp.bfloat16),
            pltpu.VMEM((latents, tokens), jnp.int32),
            pltpu.VMEM((n, latents, tokens), jnp.bfloat16),
            pltpu.VMEM((tokens, width), jnp.bfloat16),
            pltpu.VMEM((n * latents, width), jnp.bfloat16),
            pltpu.VMEM((4, 2, group, latents, half_tokens), jnp.float32),
            pltpu.VMEM((4, group, latents, half_tokens), jnp.float32),
            pltpu.VMEM((4, group, latents, half_tokens), jnp.bfloat16),
            pltpu.VMEM((2, chips, latents, half_tokens), jnp.bfloat16),
            pltpu.VMEM((2, 2 * group, latents, COLUMNS), jnp.bfloat16),
            dma((2,)), dma((DEPTHS + 1,)), dma((DEPTHS + 1,)), dma((2,)),
            dma((chips,)), dma((chips,)), dma((chips,)), dma((chips,)),
            dma((4,)), dma((4,)), dma((4, group)), dma((2, chips)),
        ],
        compiler_params=pltpu.CompilerParams(
            collective_id=0, has_side_effects=True, vmem_limit_bytes=38 * MIB
        ),
        cost_estimate=pl.CostEstimate(
            flops=4 * n * latents * tokens * width,
            bytes_accessed=2 * (2 * n * latents + tokens) * width,
            transcendentals=0,
        ),
        name="exchange",
    )(codes, mask, errors, decoders)


def encoder_kernel(held, code, mask, inputs, decoder_grad, code_grad, encoder_grad, pre, pass_sem):
    def hand_on(s):
        return pltpu.make_async_copy(held.at[s], decoder_grad.at[s], pass_sem.at[s])

    @pl.when(pl.program_id(0) == 0)
    def _():
        for s in range(held.shape[0]):
            hand_on(s).start()
        code_grad[...] = code[...]
        pre[...] = (code[...] * mask[...].astype(jnp.float32)).astype(jnp.bfloat16)

    encoder_grad[...] = jnp.dot(
        pre[...], inputs[...], preferred_element_type=jnp.float32
    ).astype(jnp.bfloat16)

    @pl.when(pl.program_id(0) == pl.num_programs(0) - 1)
    def _():
        for s in range(held.shape[0]):
            hand_on(s).wait()


def encoder(held, code, mask, inputs):
    latents, tokens = code.shape
    n, _, width = held.shape
    whole = lambda *shape: pl.BlockSpec(shape, lambda i: (0,) * len(shape))
    any_space = pl.BlockSpec(memory_space=pl.ANY)
    return pl.pallas_call(
        encoder_kernel,
        grid=(width // COLUMNS,),
        out_shape=(
            jax.ShapeDtypeStruct(held.shape, jnp.bfloat16),
            jax.ShapeDtypeStruct((latents, tokens), jnp.float32),
            jax.ShapeDtypeStruct((latents, width), jnp.bfloat16),
        ),
        in_specs=[
            any_space,
            whole(latents, tokens),
            whole(latents, tokens),
            pl.BlockSpec((tokens, COLUMNS), lambda i: (0, i)),
        ],
        out_specs=(
            any_space,
            whole(latents, tokens),
            pl.BlockSpec((latents, COLUMNS), lambda i: (0, i)),
        ),
        scratch_shapes=[
            pltpu.VMEM((latents, tokens), jnp.bfloat16),
            pltpu.SemaphoreType.DMA((n,)),
        ],
        compiler_params=pltpu.CompilerParams(vmem_limit_bytes=20 * MIB),
        cost_estimate=pl.CostEstimate(
            flops=2 * latents * tokens * width,
            bytes_accessed=2 * (2 * n * latents + tokens) * width,
            transcendentals=0,
        ),
        name="encoder",
    )(held, code, mask, inputs)


def body(saved_codes, relu_mask, errors, decoders, inputs, n):
    latents = saved_codes.shape[1]
    width = errors.shape[2]
    held, code = exchange(
        n, saved_codes[0], relu_mask[0], errors[0], decoders.reshape(n * latents, width)
    )
    decoder_grad, code_grad, encoder_grad = encoder(held, code, relu_mask[0], inputs[0])
    return decoder_grad[None], code_grad[None], encoder_grad[None]


def solution(mesh):
    return jax.shard_map(
        functools.partial(body, n=mesh.shape["layer"]),
        mesh=mesh,
        in_specs=(
            P("layer", "lat", None),
            P("layer", "lat", None),
            P("layer", None, None),
            P("layer", None, "lat", None),
            P("layer", None, None),
        ),
        out_specs=(P("layer", None, "lat", None), P("layer", "lat", None), P("layer", "lat", None)),
        check_vma=False,
    )
```

time: 50.4 us -> 39.3 us (0.78)
  the two profiles are of different devices: /device:TPU:20 before, /device:TPU:13 now
where the time goes in v2:
time: 39.3 us; the launch traced here: 39.1 us
  Pallas kernels  36.4 us (93%)
  local copies, waits for them, and re-layouts  1.99 us (5%)
  between operations  0.66 us (2%)
    pallas_call x1, Pallas kernels, exchange(): pl.pallas_call(functools.partial(exchange_kernel, n), out_shape=(jax.Shap...  29.2 us
    pallas_call x1, Pallas kernels, encoder(): pl.pallas_call(encoder_kernel, grid=(width // COLUMNS,), out_shape=(jax.S...  7.26 us
    unnamed x6, local copies, waits for them, and re-layouts  1.99 us

profile of v2, /device:TPU:13, one launch (start us, length us, event | category | flops | bytes accessed | tf_op | source)
XLA Modules:
  0.0 39.1 jit_solution(815405779593513421)
XLA Ops:
  0.6 0.0 copy-start.1
  0.6 1.0 %copy-done.1 = s32[1,128,1024]{2,1,0:T(8,128)S(1)} copy-done((s32[1,128,1024]{2,1,0:T(8,128)S(1)}, s32[1,128,1024]{2,1,0:T(8,128)}, u32[]{:S(2)}) %copy-start.1) | copy-done | bytes 524312
  1.7 0.0 copy-start.2
  1.7 0.9 %copy-done.2 = bf16[1,128,1024]{2,1,0:T(8,128)(2,1)S(1)} copy-done((bf16[1,128,1024]{2,1,0:T(8,128)(2,1)S(1)}, bf16[1,128,1024]{2,1,0:T(8,128)(2,1)}, u32[]{:S(2)}) %copy-start.2) | copy-done | bytes 262168
  2.6 0.0 copy-start
  2.6 29.2 %exchange.1 = (bf16[8,128,4096]{2,1,0:T(8,128)(2,1)S(1)}, f32[128,1024]{1,0:T(8,128)S(1)}) custom-call(bf16[128,1024]{1,0:T(8,128)(2,1)S(1)} %bitcast.11, s32[128,1024]{1,0:T(8,128)S(1)} %bitcast.9, bf16[1024,4096]{1,0:T(8,128)(2,1)} %bitcast.12, bf16[1024,4096]{1,0:T(8,128)(2,1)} %bitcast.13), custom_call_target="tpu_custom_call" | custom-call | flops 17179869184 | bytes 25165824 | tf_op jit(solution)/shard_map/exchange/pallas_call | solution.py:296
  31.8 0.0 copy-done
  31.8 7.3 %encoder.1 = (bf16[8,128,4096]{2,1,0:T(8,128)(2,1)}, f32[128,1024]{1,0:T(8,128)}, bf16[128,4096]{1,0:T(8,128)(2,1)}) custom-call(bf16[8,128,4096]{2,1,0:T(8,128)(2,1)S(1)} %get-tuple-element.8.held, f32[128,1024]{1,0:T(8,128)S(1)} %get-tuple-element.9.code, s32[128,1024]{1,0:T(8,128)S(1)} %bitcast.10, bf16[1024,4096]{1,0:T(8,128)(2,1)S(1)} %bitcast.8), custom_call_target="tpu_custom_call" | custom-call | flops 1073741824 | bytes 25165824 | tf_op jit(solution)/shard_map/encoder/pallas_call | solution.py:357
Async XLA Ops:
  0.6 1.0 %copy-start.1 = (s32[1,128,1024]{2,1,0:T(8,128)S(1)}, s32[1,128,1024]{2,1,0:T(8,128)}, u32[]{:S(2)}) copy-start(s32[1,128,1024]{2,1,0:T(8,128)} %param.6) | copy-start | bytes 1572868
  1.7 0.9 %copy-start.2 = (bf16[1,128,1024]{2,1,0:T(8,128)(2,1)S(1)}, bf16[1,128,1024]{2,1,0:T(8,128)(2,1)}, u32[]{:S(2)}) copy-start(bf16[1,128,1024]{2,1,0:T(8,128)(2,1)} %param.5) | copy-start | bytes 786436
  2.6 29.2 %copy-start = (bf16[1,1024,4096]{2,1,0:T(8,128)(2,1)S(1)}, bf16[1,1024,4096]{2,1,0:T(8,128)(2,1)}, u32[]{:S(2)}) copy-start(bf16[1,1024,4096]{2,1,0:T(8,128)(2,1)} %param.9) | copy-start | bytes 25165828

commit v3 on v2

--- a/solution.py
+++ b/solution.py
@@ -14,8 +14,8 @@
 
 
 def exchange_kernel(
-    n, codes_hbm, mask_hbm, errors_hbm, decoders_hbm, decoder_grad, code_grad,
-    codes, mask, gathered, errors, decoders, terms, twin_terms, outgoing, incoming, stage,
+    n, codes_hbm, mask_hbm, errors_hbm, decoders_hbm, inputs_hbm, decoder_grad, code_grad, encoder_grad,
+    codes, mask, gathered, errors, slab, terms, twin_terms, outgoing, incoming, stage, pre,
     load_sem, decoder_sem, error_sem, stage_sem,
     gather_send, gather_recv, relay_send, relay_recv,
     twin_send, twin_recv, term_send, term_recv,
@@ -29,12 +29,15 @@
     late = chip >= group
     _, latents, tokens = gathered.shape
     width = errors.shape[1]
+    decoders = slab.at[pl.ds(0, n * latents)]
+    inputs = slab.at[pl.ds(0, tokens)]
     half_rows = 2 * group * latents
     half_tokens = tokens // 2
     depth = width // DEPTHS
 
     load_codes = pltpu.make_async_copy(codes_hbm, codes, load_sem.at[0])
     load_mask = pltpu.make_async_copy(mask_hbm, mask, load_sem.at[1])
+    load_inputs = pltpu.make_async_copy(inputs_hbm, inputs, load_sem.at[2])
 
     def load_errors(k):
         part = (pl.ds(half_tokens, half_tokens), slice(None))
@@ -185,6 +188,8 @@
                     take_active(source).wait_recv()
                     relay(source).start()
 
+    load_inputs.start()
+
     blocks = width // COLUMNS
 
     def put(first, i, slot):
@@ -193,7 +198,14 @@
             stage.at[slot], decoder_grad.at[pl.ds(first, 2 * group), :, columns], stage_sem.at[slot]
         )
 
-    def decoder_rows(first, late_sum):
+    def relay_far():
+        for source in range(group):
+            @pl.when(source < chip - 1)
+            def _():
+                take_active(source).wait_recv()
+                relay(source).start()
+
+    def decoder_rows(first, near):
         @pl.loop(0, blocks)
         def _(i):
             slot = lax.rem(i, 2)
@@ -210,10 +222,14 @@
             for s in range(2 * group):
                 stage[slot, s] = jnp.where(first + s <= me, products[s], 0.0).astype(jnp.bfloat16)
             put(first, i, slot).start()
-            if late_sum:
+            if near:
                 @pl.when(i == 0)
                 def _():
                     pair_sum(3)
+
+                @pl.when(i == blocks - 3)
+                def _():
+                    relay_far()
 
         put(first, blocks - 2, (blocks - 2) % 2).wait()
         put(first, blocks - 1, (blocks - 1) % 2).wait()
@@ -225,17 +241,17 @@
         for i in range(blocks):
             put(2 * group, i, 0).start()
 
-    for source in range(chips):
-        @pl.when(source < chip - 1)
-        def _():
-            take_active(source).wait_recv()
-            relay(source).start()
-
     take_relay(chip).wait_recv()
 
     @pl.when(late)
     def _():
         for source in range(group, chips):
+            @pl.when(source < chip - 1)
+            def _():
+                take_active(source).wait_recv()
+                relay(source).start()
+
+        for source in range(group, chips):
             @pl.when(source < chip)
             def _():
                 take_relay(source).wait_recv()
@@ -243,6 +259,7 @@
 
     @pl.when(jnp.logical_not(late))
     def _():
+        relay_far()
         for i in range(blocks):
             put(2 * group, i, 0).wait()
 
@@ -264,6 +281,16 @@
                 take_term(q, source).wait_recv()
                 code_grad[:, columns] += incoming[q, source].astype(jnp.float32)
 
+    pre[...] = (code_grad[...] * mask[...].astype(jnp.float32)).astype(jnp.bfloat16)
+    load_inputs.wait()
+
+    @pl.loop(0, blocks)
+    def _(i):
+        columns = pl.ds(pl.multiple_of(i * COLUMNS, COLUMNS), COLUMNS)
+        encoder_grad[:, columns] = jnp.dot(
+            pre[...], inputs[:, columns], preferred_element_type=jnp.float32
+        ).astype(jnp.bfloat16)
+
     relay(chip).wait_send()
     for other in range(chips):
         @pl.when(other < chip)
@@ -285,7 +312,7 @@
             send_twin(m).wait_send()
 
 
-def exchange(n, codes, mask, errors, decoders):
+def exchange(n, codes, mask, errors, decoders, inputs):
     latents, tokens = codes.shape
     width = errors.shape[1]
     chips = n // 2
@@ -298,103 +325,68 @@
         out_shape=(
             jax.ShapeDtypeStruct((n, latents, width), jnp.bfloat16),
             jax.ShapeDtypeStruct((latents, tokens), jnp.float32),
+            jax.ShapeDtypeStruct((latents, width), jnp.bfloat16),
         ),
-        in_specs=[any_space] * 4,
-        out_specs=(any_space, pl.BlockSpec(memory_space=pltpu.VMEM)),
+        in_specs=[any_space] * 5,
+        out_specs=(any_space,) + (pl.BlockSpec(memory_space=pltpu.VMEM),) * 2,
         scratch_shapes=[
             pltpu.VMEM((latents, tokens), jnp.bfloat16),
             pltpu.VMEM((latents, tokens), jnp.int32),
             pltpu.VMEM((n, latents, tokens), jnp.bfloat16),
             pltpu.VMEM((tokens, width), jnp.bfloat16),
-            pltpu.VMEM((n * latents, width), jnp.bfloat16),
+            pltpu.VMEM((max(n * latents, tokens), width), jnp.bfloat16),
             pltpu.VMEM((4, 2, group, latents, half_tokens), jnp.float32),
             pltpu.VMEM((4, group, latents, half_tokens), jnp.float32),
             pltpu.VMEM((4, group, latents, half_tokens), jnp.bfloat16),
             pltpu.VMEM((2, chips, latents, half_tokens), jnp.bfloat16),
             pltpu.VMEM((2, 2 * group, latents, COLUMNS), jnp.bfloat16),
-            dma((2,)), dma((DEPTHS + 1,)), dma((DEPTHS + 1,)), dma((2,)),
+            pltpu.VMEM((latents, tokens), jnp.bfloat16),
+            dma((3,)), dma((DEPTHS + 1,)), dma((DEPTHS + 1,)), dma((2,)),
             dma((chips,)), dma((chips,)), dma((chips,)), dma((chips,)),
             dma((4,)), dma((4,)), dma((4, group)), dma((2, chips)),
         ],
         compiler_params=pltpu.CompilerParams(
-            collective_id=0, has_side_effects=True, vmem_limit_bytes=38 * MIB
+            collective_id=0, has_side_effects=True, vmem_limit_bytes=40 * MIB
         ),
         cost_estimate=pl.CostEstimate(
-            flops=4 * n * latents * tokens * width,
+            flops=(4 * n + 2) * latents * tokens * width,
             bytes_accessed=2 * (2 * n * latents + tokens) * width,
             transcendentals=0,
         ),
         name="exchange",
-    )(codes, mask, errors, decoders)
-
-
-def encoder_kernel(held, code, mask, inputs, decoder_grad, code_grad, encoder_grad, pre, pass_sem):
-    def hand_on(s):
-        return pltpu.make_async_copy(held.at[s], decoder_grad.at[s], pass_sem.at[s])
-
-    @pl.when(pl.program_id(0) == 0)
-    def _():
-        for s in range(held.shape[0]):
-            hand_on(s).start()
-        code_grad[...] = code[...]
-        pre[...] = (code[...] * mask[...].astype(jnp.float32)).astype(jnp.bfloat16)
-
-    encoder_grad[...] = jnp.dot(
-        pre[...], inputs[...], preferred_element_type=jnp.float32
-    ).astype(jnp.bfloat16)
-
-    @pl.when(pl.program_id(0) == pl.num_programs(0) - 1)
-    def _():
-        for s in range(held.shape[0]):
-            hand_on(s).wait()
-
-
-def encoder(held, code, mask, inputs):
-    latents, tokens = code.shape
-    n, _, width = held.shape
-    whole = lambda *shape: pl.BlockSpec(shape, lambda i: (0,) * len(shape))
+    )(codes, mask, errors, decoders, inputs)
+
+
+def hand_on_kernel(*refs):
+    count = (len(refs) - 1) // 2
+    sems = refs[-1]
+    copies = [pltpu.make_async_copy(refs[i], refs[count + i], sems.at[i]) for i in range(count)]
+    for copy in copies:
+        copy.start()
+    for copy in copies:
+        copy.wait()
+
+
+def hand_on(*arrays):
     any_space = pl.BlockSpec(memory_space=pl.ANY)
     return pl.pallas_call(
-        encoder_kernel,
-        grid=(width // COLUMNS,),
-        out_shape=(
-            jax.ShapeDtypeStruct(held.shape, jnp.bfloat16),
-            jax.ShapeDtypeStruct((latents, tokens), jnp.float32),
-            jax.ShapeDtypeStruct((latents, width), jnp.bfloat16),
-        ),
-        in_specs=[
-            any_space,
-            whole(latents, tokens),
-            whole(latents, tokens),
-            pl.BlockSpec((tokens, COLUMNS), lambda i: (0, i)),
-        ],
-        out_specs=(
-            any_space,
-            whole(latents, tokens),
-            pl.BlockSpec((latents, COLUMNS), lambda i: (0, i)),
-        ),
-        scratch_shapes=[
-            pltpu.VMEM((latents, tokens), jnp.bfloat16),
-            pltpu.SemaphoreType.DMA((n,)),
-        ],
-        compiler_params=pltpu.CompilerParams(vmem_limit_bytes=20 * MIB),
-        cost_estimate=pl.CostEstimate(
-            flops=2 * latents * tokens * width,
-            bytes_accessed=2 * (2 * n * latents + tokens) * width,
-            transcendentals=0,
-        ),
-        name="encoder",
-    )(held, code, mask, inputs)
+        hand_on_kernel,
+        out_shape=tuple(jax.ShapeDtypeStruct(a.shape, a.dtype) for a in arrays),
+        in_specs=[any_space] * len(arrays),
+        out_specs=(any_space,) * len(arrays),
+        scratch_shapes=[pltpu.SemaphoreType.DMA((len(arrays),))],
+        compiler_params=pltpu.CompilerParams(vmem_limit_bytes=MIB),
+        name="hand_on",
+    )(*arrays)
 
 
 def body(saved_codes, relu_mask, errors, decoders, inputs, n):
     latents = saved_codes.shape[1]
     width = errors.shape[2]
-    held, code = exchange(
-        n, saved_codes[0], relu_mask[0], errors[0], decoders.reshape(n * latents, width)
+    held = exchange(
+        n, saved_codes[0], relu_mask[0], errors[0], decoders.reshape(n * latents, width), inputs[0]
     )
-    decoder_grad, code_grad, encoder_grad = encoder(held, code, relu_mask[0], inputs[0])
-    return decoder_grad[None], code_grad[None], encoder_grad[None]
+    return tuple(result[None] for result in hand_on(*held))
 
 
 def solution(mesh):

time: 39.3 us -> 38.6 us (0.982)
  Pallas kernels: 36.4 us -> 35.8 us
    pallas_call x1, Pallas kernels: 7.26 us -> 3.92 us  [hand_on(): pl.pallas_call(hand_on_kernel, out_shape=tuple((jax.ShapeDtypeStruct(a.sh...]
    pallas_call x1, Pallas kernels: 29.2 us -> 31.9 us  [exchange(): pl.pallas_call(functools.partial(exchange_kernel, n), out_shape=(jax.Shap...]
    unnamed x6 -> x4, local copies, waits for them, and re-layouts: 1.99 us -> 1.98 us
where the time goes in v3:
time: 38.6 us; the launch traced here: 38.4 us
  Pallas kernels  35.8 us (93%)
  local copies, waits for them, and re-layouts  1.98 us (5%)
  between operations  0.65 us (2%)
    pallas_call x1, Pallas kernels, exchange(): pl.pallas_call(functools.partial(exchange_kernel, n), out_shape=(jax.Shap...  31.9 us
    pallas_call x1, Pallas kernels, hand_on(): pl.pallas_call(hand_on_kernel, out_shape=tuple((jax.ShapeDtypeStruct(a.sh...  3.92 us
    unnamed x4, local copies, waits for them, and re-layouts  1.98 us

profile of v3, /device:TPU:13, one launch (start us, length us, event | category | flops | bytes accessed | tf_op | source)
XLA Modules:
  0.0 38.4 jit_solution(4891015876292646368)
XLA Ops:
  0.6 0.0 copy-start
  0.6 1.0 %copy-done = s32[1,128,1024]{2,1,0:T(8,128)S(1)} copy-done((s32[1,128,1024]{2,1,0:T(8,128)S(1)}, s32[1,128,1024]{2,1,0:T(8,128)}, u32[]{:S(2)}) %copy-start) | copy-done | bytes 524312
  1.7 0.0 copy-start.1
  1.7 0.9 %copy-done.1 = bf16[1,128,1024]{2,1,0:T(8,128)(2,1)S(1)} copy-done((bf16[1,128,1024]{2,1,0:T(8,128)(2,1)S(1)}, bf16[1,128,1024]{2,1,0:T(8,128)(2,1)}, u32[]{:S(2)}) %copy-start.1) | copy-done | bytes 262168
  2.6 31.9 %exchange.1 = (bf16[8,128,4096]{2,1,0:T(8,128)(2,1)S(1)}, f32[128,1024]{1,0:T(8,128)S(1)}, bf16[128,4096]{1,0:T(8,128)(2,1)S(1)}) custom-call(bf16[128,1024]{1,0:T(8,128)(2,1)S(1)} %bitcast.9, s32[128,1024]{1,0:T(8,128)S(1)} %bitcast.8, bf16[1024,4096]{1,0:T(8,128)(2,1)} %bitcast.10, bf16[1024,4096]{1,0:T(8,128)(2,1)} %bitcast.11, bf16[1024,4096]{1,0:T(8,128)(2,1)} %bitcast.12), custom_call_target="tpu_custom_call" | custom-call | flops 18253611008 | bytes 25165824 | tf_op jit(solution)/shard_map/exchange/pallas_call | solution.py:323
  34.5 3.9 %hand_on.1 = (bf16[8,128,4096]{2,1,0:T(8,128)(2,1)}, f32[128,1024]{1,0:T(8,128)}, bf16[128,4096]{1,0:T(8,128)(2,1)}) custom-call(bf16[8,128,4096]{2,1,0:T(8,128)(2,1)S(1)} %get-tuple-element.9.refs_0_, f32[128,1024]{1,0:T(8,128)S(1)} %get-tuple-element.10.refs_1_, bf16[128,4096]{1,0:T(8,128)(2,1)S(1)} %get-tuple-element.11.refs_2_), custom_call_target="tpu_custom_call" | custom-call | tf_op jit(solution)/shard_map/hand_on/pallas_call | solution.py:372
Async XLA Ops:
  0.6 1.0 %copy-start = (s32[1,128,1024]{2,1,0:T(8,128)S(1)}, s32[1,128,1024]{2,1,0:T(8,128)}, u32[]{:S(2)}) copy-start(s32[1,128,1024]{2,1,0:T(8,128)} %param.6) | copy-start | bytes 1572868
  1.7 0.9 %copy-start.1 = (bf16[1,128,1024]{2,1,0:T(8,128)(2,1)S(1)}, bf16[1,128,1024]{2,1,0:T(8,128)(2,1)}, u32[]{:S(2)}) copy-start(bf16[1,128,1024]{2,1,0:T(8,128)(2,1)} %param.5) | copy-start | bytes 786436

commit v4 on v3

--- a/solution.py
+++ b/solution.py
@@ -8,7 +8,7 @@
 from jax.sharding import PartitionSpec as P
 
 MESH = pl.DeviceIdType.MESH
-DEPTHS = 4
+DEPTHS = 2
 COLUMNS = 512
 MIB = 1 << 20
 
@@ -46,9 +46,7 @@
         return pltpu.make_async_copy(errors_hbm.at[part], errors.at[part], error_sem.at[k])
 
     def load_decoders(k):
-        part = (pl.ds(half_rows, half_rows), slice(None))
-        if k < DEPTHS:
-            part = (pl.ds(0, half_rows), pl.ds(k * depth, depth))
+        part = (slice(None), pl.ds(k * depth, depth))
         return pltpu.make_async_copy(decoders_hbm.at[part], decoders.at[part], decoder_sem.at[k])
 
     load_codes.start()
@@ -57,11 +55,6 @@
         load_errors(k).start()
         load_decoders(k).start()
     load_errors(DEPTHS).start()
-
-    @pl.when(late)
-    def _():
-        load_decoders(DEPTHS).start()
-
     barrier = pltpu.get_barrier_semaphore()
     pl.semaphore_signal(barrier, inc=1, device_id={"layer": twin}, device_id_type=MESH)
     for other in range(chips):
@@ -143,50 +136,49 @@
                 outgoing[m, place] = total.astype(jnp.bfloat16)
                 send_term(m, place).start()
 
-    steps = jnp.where(late, 4, 2)
-
-    @pl.loop(0, steps)
-    def _(m):
-        @pl.when(m == 1)
-        def _():
-            load_errors(DEPTHS).wait()
-
-        @pl.when(m == 2)
-        def _():
-            load_decoders(DEPTHS).wait()
-
-        rows = pl.ds(pl.multiple_of((m // 2) * half_rows, half_rows), half_rows)
-        part = pl.ds(pl.multiple_of(lax.rem(m, 2) * half_tokens, half_tokens), half_tokens)
-        for k in range(DEPTHS):
-            @pl.when(m == 0)
-            def _():
+    def products(part, columns):
+        return lax.dot_general(
+            decoders[:, columns], errors[part, columns],
+            (((1,), (1,)), ((), ())),
+            preferred_element_type=jnp.float32,
+        ).reshape(2, group, 2, latents, half_tokens)
+
+    for q in range(2):
+        part = pl.ds(q * half_tokens, half_tokens)
+        if q == 0:
+            for k in range(DEPTHS):
                 load_errors(k).wait()
                 load_decoders(k).wait()
-
-            columns = pl.ds(k * depth, depth)
-            product = lax.dot_general(
-                decoders[rows, columns], errors[part, columns],
-                (((1,), (1,)), ((), ())),
-                preferred_element_type=jnp.float32,
-            ).reshape(group, 2, latents, half_tokens)
-            for parity in range(2):
-                if k == 0:
-                    terms[m, parity] = product[:, parity]
-                else:
-                    terms[m, parity] += product[:, parity]
-        send_twin(m).start()
-
-        @pl.when(m >= 1)
-        def _():
-            pair_sum(m - 1)
-
-        @pl.when(m == 1)
-        def _():
-            for source in range(chips):
-                @pl.when(source == chip - 1)
-                def _():
-                    take_active(source).wait_recv()
-                    relay(source).start()
+                product = products(part, pl.ds(k * depth, depth))
+                for half in range(2):
+                    for parity in range(2):
+                        if k == 0:
+                            terms[2 * half, parity] = product[half, :, parity]
+                        else:
+                            terms[2 * half, parity] += product[half, :, parity]
+        else:
+            load_errors(DEPTHS).wait()
+            product = products(part, slice(None))
+            for half in range(2):
+                for parity in range(2):
+                    terms[2 * half + 1, parity] = product[half, :, parity]
+        send_twin(q).start()
+
+        @pl.when(late)
+        def _():
+            send_twin(2 + q).start()
+
+    pair_sum(0)
+
+    @pl.when(late)
+    def _():
+        pair_sum(2)
+
+    for source in range(chips):
+        @pl.when(source == chip - 1)
+        def _():
+            take_active(source).wait_recv()
+            relay(source).start()
 
     load_inputs.start()
 
@@ -225,6 +217,7 @@
             if near:
                 @pl.when(i == 0)
                 def _():
+                    pair_sum(1)
                     pair_sum(3)
 
                 @pl.when(i == blocks - 3)
@@ -341,7 +334,7 @@
             pltpu.VMEM((2, chips, latents, half_tokens), jnp.bfloat16),
             pltpu.VMEM((2, 2 * group, latents, COLUMNS), jnp.bfloat16),
             pltpu.VMEM((latents, tokens), jnp.bfloat16),
-            dma((3,)), dma((DEPTHS + 1,)), dma((DEPTHS + 1,)), dma((2,)),
+            dma((3,)), dma((DEPTHS,)), dma((DEPTHS + 1,)), dma((2,)),
             dma((chips,)), dma((chips,)), dma((chips,)), dma((chips,)),
             dma((4,)), dma((4,)), dma((4, group)), dma((2, chips)),
         ],
@@ -360,7 +353,13 @@
 def hand_on_kernel(*refs):
     count = (len(refs) - 1) // 2
     sems = refs[-1]
-    copies = [pltpu.make_async_copy(refs[i], refs[count + i], sems.at[i]) for i in range(count)]
+    pieces = []
+    for source, target in zip(refs[:count], refs[count:-1]):
+        if len(source.shape) == 3:
+            pieces += [(source.at[i], target.at[i]) for i in range(source.shape[0])]
+        else:
+            pieces.append((source, target))
+    copies = [pltpu.make_async_copy(*piece, sems.at[i]) for i, piece in enumerate(pieces)]
     for copy in copies:
         copy.start()
     for copy in copies:
@@ -374,7 +373,7 @@
         out_shape=tuple(jax.ShapeDtypeStruct(a.shape, a.dtype) for a in arrays),
         in_specs=[any_space] * len(arrays),
         out_specs=(any_space,) * len(arrays),
-        scratch_shapes=[pltpu.SemaphoreType.DMA((len(arrays),))],
+        scratch_shapes=[pltpu.SemaphoreType.DMA((arrays[0].shape[0] + len(arrays),))],
         compiler_params=pltpu.CompilerParams(vmem_limit_bytes=MIB),
         name="hand_on",
     )(*arrays)
@@ -383,9 +382,8 @@
 def body(saved_codes, relu_mask, errors, decoders, inputs, n):
     latents = saved_codes.shape[1]
     width = errors.shape[2]
-    held = exchange(
-        n, saved_codes[0], relu_mask[0], errors[0], decoders.reshape(n * latents, width), inputs[0]
-    )
+    operands = (saved_codes[0], relu_mask[0], errors[0], decoders.reshape(n * latents, width), inputs[0])
+    held = exchange(n, *(pltpu.with_memory_space_constraint(x, pltpu.HBM) for x in operands))
     return tuple(result[None] for result in hand_on(*held))
 
 

time: 38.6 us -> 36.7 us (0.951)
  the two profiles are of different devices: /device:TPU:13 before, /device:TPU:7 now
where the time goes in v4:
time: 36.7 us; the launch traced here: 36.6 us
  Pallas kernels  35.9 us (98%)
  between operations  0.64 us (2%)
    pallas_call x1, Pallas kernels, exchange(): pl.pallas_call(functools.partial(exchange_kernel, n), out_shape=(jax.Shap...  32.1 us
    pallas_call x1, Pallas kernels, hand_on(): pl.pallas_call(hand_on_kernel, out_shape=tuple((jax.ShapeDtypeStruct(a.sh...  3.87 us

profile of v4, /device:TPU:7, one launch (start us, length us, event | category | flops | bytes accessed | tf_op | source)
XLA Modules:
  0.0 36.6 jit_solution(14473230426919168190)
XLA Ops:
  0.6 32.1 %exchange.1 = (bf16[8,128,4096]{2,1,0:T(8,128)(2,1)S(1)}, f32[128,1024]{1,0:T(8,128)S(1)}, bf16[128,4096]{1,0:T(8,128)(2,1)S(1)}) custom-call(bf16[128,1024]{1,0:T(8,128)(2,1)} %bitcast.15, s32[128,1024]{1,0:T(8,128)} %bitcast.13, bf16[1024,4096]{1,0:T(8,128)(2,1)} %bitcast.8, bf16[1024,4096]{1,0:T(8,128)(2,1)} %bitcast.9, bf16[1024,4096]{1,0:T(8,128)(2,1)} %bitcast.10), custom_call_target="tpu_custom_call" | custom-call | flops 18253611008 | bytes 25165824 | tf_op jit(solution)/shard_map/exchange/pallas_call | solution.py:316
  32.7 3.9 %hand_on.1 = (bf16[8,128,4096]{2,1,0:T(8,128)(2,1)}, f32[128,1024]{1,0:T(8,128)}, bf16[128,4096]{1,0:T(8,128)(2,1)}) custom-call(bf16[8,128,4096]{2,1,0:T(8,128)(2,1)S(1)} %get-tuple-element.9.refs_0_, f32[128,1024]{1,0:T(8,128)S(1)} %get-tuple-element.10.refs_1_, bf16[128,4096]{1,0:T(8,128)(2,1)S(1)} %get-tuple-element.11.refs_2_), custom_call_target="tpu_custom_call" | custom-call | tf_op jit(solution)/shard_map/hand_on/pallas_call | solution.py:371

commit v5 on v4

--- a/solution.py
+++ b/solution.py
@@ -9,7 +9,7 @@
 
 MESH = pl.DeviceIdType.MESH
 DEPTHS = 2
-COLUMNS = 512
+COLUMNS = 1024
 MIB = 1 << 20
 
 

time: 36.7 us -> 34.8 us (0.948)
  Pallas kernels: 35.9 us -> 34 us
    pallas_call x1, Pallas kernels: 32.1 us -> 30.1 us  [exchange(): pl.pallas_call(functools.partial(exchange_kernel, n), out_shape=(jax.Shap...]
where the time goes in v5:
time: 34.8 us; the launch traced here: 34.6 us
  Pallas kernels  34 us (98%)
  between operations  0.64 us (2%)
    pallas_call x1, Pallas kernels, exchange(): pl.pallas_call(functools.partial(exchange_kernel, n), out_shape=(jax.Shap...  30.1 us
    pallas_call x1, Pallas kernels, hand_on(): pl.pallas_call(hand_on_kernel, out_shape=tuple((jax.ShapeDtypeStruct(a.sh...  3.87 us

profile of v5, /device:TPU:7, one launch (start us, length us, event | category | flops | bytes accessed | tf_op | source)
XLA Modules:
  0.0 34.6 jit_solution(10170812030605853866)
XLA Ops:
  0.6 30.1 %exchange.1 = (bf16[8,128,4096]{2,1,0:T(8,128)(2,1)S(1)}, f32[128,1024]{1,0:T(8,128)S(1)}, bf16[128,4096]{1,0:T(8,128)(2,1)S(1)}) custom-call(bf16[128,1024]{1,0:T(8,128)(2,1)} %bitcast.15, s32[128,1024]{1,0:T(8,128)} %bitcast.13, bf16[1024,4096]{1,0:T(8,128)(2,1)} %bitcast.8, bf16[1024,4096]{1,0:T(8,128)(2,1)} %bitcast.9, bf16[1024,4096]{1,0:T(8,128)(2,1)} %bitcast.10), custom_call_target="tpu_custom_call" | custom-call | flops 18253611008 | bytes 25165824 | tf_op jit(solution)/shard_map/exchange/pallas_call | solution.py:316
  30.8 3.9 %hand_on.1 = (bf16[8,128,4096]{2,1,0:T(8,128)(2,1)}, f32[128,1024]{1,0:T(8,128)}, bf16[128,4096]{1,0:T(8,128)(2,1)}) custom-call(bf16[8,128,4096]{2,1,0:T(8,128)(2,1)S(1)} %get-tuple-element.9.refs_0_, f32[128,1024]{1,0:T(8,128)S(1)} %get-tuple-element.10.refs_1_, bf16[128,4096]{1,0:T(8,128)(2,1)S(1)} %get-tuple-element.11.refs_2_), custom_call_target="tpu_custom_call" | custom-call | tf_op jit(solution)/shard_map/hand_on/pallas_call | solution.py:371
